TPU v7x, 256 devices: a whole 4x4x8 slice. The times are simulated.
256 devices in a mesh: pair: 32 (over x, z), aux: 8 (over y, core).
Axes of the slice: x: 4, y: 4, z: 8, core: 2. Of those that a mesh axis runs over, the one named last changes fastest.
Arguments:
- three_centre: bfloat16 [32, 128, 1024, 128], P('pair', None, 'aux'), may hold values from -6 to 6
- green_occ: bfloat16 [160, 128, 128], P('pair'), may hold values from -0.5 to 0.5
- green_virt: bfloat16 [160, 128, 128], P('pair'), may hold values from -0.5 to 0.5
- tile_home: int32 [160], replicated, may hold values from 0 to 159, as said below
- term_source: int32 [32, 7], P('pair'), may hold values from 0 to 2
- term_occ: int32 [32, 7], P('pair'), may hold values from 0 to 159, as said below
- term_virt: int32 [32, 7], P('pair'), may hold values from 0 to 159, as said below
- term_count: int32 [32], P('pair'), may hold values from 2 to 7, as said below
Outputs:
- polarizability: float32 [1024, 1024], P('aux', 'pair')
Inputs may be any that keep to these rules, and one draw needn't show every extreme that they name: A permutation: tile id t is stored at row tile_home[t] of green_occ and of green_virt. `term_occ`: counting the occupied and virtual ids of all terms of the 1 block of one pair index together, at most 2 are stored on any one owner (row tile_home[id] lies in owner tile_home[id] // 5); one owner receives exactly 2 from every pair index. Ids in slots at or beyond term_count are valid but unused. `term_virt`: counted together with term_occ as stated there. `term_count`: slots at or beyond this count contribute nothing.
All inputs are finite; a program needn't handle non-finite values.
Results may differ from a plain program's by a relative error of at most 0.0041.
Values may be sent and summed in bfloat16 or wider, within the bound.
A program may use at most 128 MiB of HBM per device.

v0:
```python
import math

import jax
import jax.numpy as jnp
from jax import lax
from jax.sharding import PartitionSpec as P


def padded(block, sides, width):
    for axis, dim in sides:
        count = lax.axis_size(axis)
        forward = [(i, i + 1) for i in range(count - 1)]
        forward.append((count - 1, 0))
        backward = [(target, source) for source, target in forward]
        low = lax.ppermute(
            lax.slice_in_dim(block, block.shape[dim] - width, None, axis=dim), axis, forward
        )
        high = lax.ppermute(lax.slice_in_dim(block, 0, width, axis=dim), axis, backward)
        block = jnp.concatenate([low, block, high], axis=dim)
    return block


def body(
    three_centre, green_occ, green_virt, tile_home, term_source, term_occ, term_virt, term_count
):
    block_count = three_centre.shape[0]
    block_size = three_centre.shape[1]
    aux_local = three_centre.shape[2]
    slot_total = term_occ.shape[1]
    pair_size = lax.axis_size("pair")
    storage_occ = tile_home[term_occ]
    storage_virt = tile_home[term_virt]
    every_occ, every_virt = (
        lax.all_gather(green_occ, "pair", axis=0, tiled=True),
        lax.all_gather(green_virt, "pair", axis=0, tiled=True),
    )
    occ_tiles = every_occ[storage_occ]
    virt_tiles = every_virt[storage_virt]
    regrouped_blocks = lax.all_to_all(three_centre, "aux", split_axis=1, concat_axis=2, tiled=True)
    haloed = padded(three_centre, (("pair", 0),), 1)
    live_mask = (jnp.arange(slot_total, dtype=jnp.int32)[None, :] < term_count[:, None]).astype(
        jnp.bfloat16
    )
    virt_tiles = virt_tiles * live_mask[:, :, None, None]
    positions = jnp.arange(block_count, dtype=jnp.int32)

    def add_term(slot_index, accumulated):
        source_index = positions + term_source[:, slot_index]
        source_blocks = haloed[source_index]
        half_product = jnp.einsum(
            "blm,blps->bmps",
            occ_tiles[:, slot_index],
            source_blocks,
            preferred_element_type=jnp.float32,
        ).astype(jnp.bfloat16)
        return accumulated + jnp.einsum(
            "bmps,bsn->bmpn",
            half_product,
            virt_tiles[:, slot_index],
            preferred_element_type=jnp.float32,
        )

    start = jnp.zeros((block_count, block_size, aux_local, block_size), jnp.float32)
    products = lax.fori_loop(0, slot_total, add_term, start).astype(jnp.bfloat16)
    regrouped_products = lax.all_to_all(products, "aux", split_axis=1, concat_axis=2, tiled=True)
    prefactor = -1.0 / (block_size * math.sqrt(block_count * pair_size * slot_total))
    partial_sum = (
        jnp.einsum(
            "bmpn,bmqn->pq",
            regrouped_products,
            regrouped_blocks,
            preferred_element_type=jnp.float32,
        )
        * prefactor
    )
    columns = lax.psum_scatter(partial_sum, "pair", scatter_dimension=1, tiled=True)
    polarizability = lax.psum_scatter(columns, "aux", scatter_dimension=0, tiled=True)
    return polarizability


def solution(mesh):
    in_specs = (
        P("pair", None, "aux", None),
        P("pair", None, None),
        P("pair", None, None),
        P(),
        P("pair", None),
        P("pair", None),
        P("pair", None),
        P("pair"),
    )
    out_specs = P("aux", "pair")
    return jax.shard_map(body, mesh=mesh, in_specs=in_specs, out_specs=out_specs, check_vma=False)
```

profile of v0, /device:TPU:2, one launch (start us, length us, event | category | flops | bytes accessed | tf_op | source)
XLA Modules:
  0.0 734.3 jit_solution(14619548804810483586)
XLA Ops:
  8.0 6.9 copy.14
  14.9 1.9 collective-permute-start
  16.8 3.9 collective-permute-start.1
  20.7 4.9 all-to-all-start.1
  27.7 111.2 %collective-permute-done = bf16[1,128,128,128]{3,1,2,0:T(8,128)(2,1)} collective-permute-done((bf16[1,128,128,128]{3,1,2,0:T(8,128)(2,1)}, bf16[1,128,128,128]{3,1,2,0:T(8,128)(2,1)}, u32[]{:S(2)}, u32[]{:S(2)}) %collective-permute-start) | collective-permute-done | bytes 4194336 | tf_op jit(solution)/shard_map/ppermute | solution.py:15
  140.1 10.5 %pad_maximum_fusion = bf16[3,128,128,128]{3,1,2,0:T(8,128)(2,1)} fusion(bf16[1,128,128,128]{3,1,2,0:T(8,128)(2,1)} %collective-permute-done.1, bf16[1,128,128,128]{3,1,2,0:T(8,128)(2,1)} %copy.14, bf16[1,128,128,128]{3,1,2,0:T(8,128)(2,1)} %collective-permute-done), kind=kLoop, calls=%fused_computation.18 | loop fusion | flops 12582912 | bytes 25165824 | tf_op jit(solution)/shard_map/concatenate | solution.py:19
  150.6 3.1 gather_fusion.3
  153.8 79.2 %all-gather.3.cloned.1.call-done = bf16[160,128,128]{2,1,0:T(8,128)(2,1)} async-done(((bf16[5,128,128]{2,1,0:T(8,128)(2,1)}), bf16[160,128,128]{2,1,0:T(8,128)(2,1)}) %all-gather.3.cloned.1.call-update) | async-done | bytes 5242896 | tf_op jit(solution)/shard_map/all_gather | solution.py:34
  232.9 3.1 gather_fusion.1
  236.0 170.1 %while.15 = (s32[]{:T(128)}, f32[1,128,128,128]{3,2,1,0:T(8,128)}, bf16[1,7,128,128]{3,2,1,0:T(8,128)(2,1)S(1)}, s32[1,7]{1,0:T(1,128)S(1)}, bf16[3,128,128,128]...) while((s32[]{:T(128)}, f32[1,128,128,128]{3,2,1,0:T(8,128)}, ...), condition=%wide.region_1.0_spmd.clone, body=%wide.region_0.0_spmd.clone.sunk | while | flops 1080033280 | bytes 29426848 | solution.py:64
  238.6 5.5 fusion.31
  244.1 14.2 %bitcast_add_fusion.2 = f32[1,128,128,128]{3,2,1,0:T(8,128)} fusion(f32[1,128,128,128]{3,2,1,0:T(8,128)} %get-tuple-element.213, pred[]{:T(512)S(6)} %compare.4, bf16[128,128,128]{2,0,1:T(8,128)(2,1)} %fusion.31, bf16[1,7,128,128]{3,2,1,0:T(8,128)(2,1)S(1)} %get-tuple-element.227, s32[]{:T(128)} %get-tuple-element.212), kind=kOutput, calls=%fused_computation.4.clone.1 | convolution fusion | flops 541065216 | bytes 21004292 | tf_op jit(solution)/shard_map/while/body/eval_jaxpr/bmps,bsn->bmpn/dot_general | solution.py:56
  260.8 5.5 fusion.31
  266.3 16.6 %bitcast_add_fusion.2 = f32[1,128,128,128]{3,2,1,0:T(8,128)} fusion(f32[1,128,128,128]{3,2,1,0:T(8,128)} %get-tuple-element.213, pred[]{:T(512)S(6)} %compare.4, bf16[128,128,128]{2,0,1:T(8,128)(2,1)} %fusion.31, bf16[1,7,128,128]{3,2,1,0:T(8,128)(2,1)S(1)} %get-tuple-element.227, s32[]{:T(128)} %get-tuple-element.212), kind=kOutput, calls=%fused_computation.4.clone.1 | convolution fusion | flops 541065216 | bytes 21004292 | tf_op jit(solution)/shard_map/while/body/eval_jaxpr/bmps,bsn->bmpn/dot_general | solution.py:56
  285.5 5.5 fusion.31
  290.9 16.6 %bitcast_add_fusion.2 = f32[1,128,128,128]{3,2,1,0:T(8,128)} fusion(f32[1,128,128,128]{3,2,1,0:T(8,128)} %get-tuple-element.213, pred[]{:T(512)S(6)} %compare.4, bf16[128,128,128]{2,0,1:T(8,128)(2,1)} %fusion.31, bf16[1,7,128,128]{3,2,1,0:T(8,128)(2,1)S(1)} %get-tuple-element.227, s32[]{:T(128)} %get-tuple-element.212), kind=kOutput, calls=%fused_computation.4.clone.1 | convolution fusion | flops 541065216 | bytes 21004292 | tf_op jit(solution)/shard_map/while/body/eval_jaxpr/bmps,bsn->bmpn/dot_general | solution.py:56
  310.1 5.5 fusion.31
  315.6 16.6 %bitcast_add_fusion.2 = f32[1,128,128,128]{3,2,1,0:T(8,128)} fusion(f32[1,128,128,128]{3,2,1,0:T(8,128)} %get-tuple-element.213, pred[]{:T(512)S(6)} %compare.4, bf16[128,128,128]{2,0,1:T(8,128)(2,1)} %fusion.31, bf16[1,7,128,128]{3,2,1,0:T(8,128)(2,1)S(1)} %get-tuple-element.227, s32[]{:T(128)} %get-tuple-element.212), kind=kOutput, calls=%fused_computation.4.clone.1 | convolution fusion | flops 541065216 | bytes 21004292 | tf_op jit(solution)/shard_map/while/body/eval_jaxpr/bmps,bsn->bmpn/dot_general | solution.py:56
  334.8 5.5 fusion.31
  340.2 16.6 %bitcast_add_fusion.2 = f32[1,128,128,128]{3,2,1,0:T(8,128)} fusion(f32[1,128,128,128]{3,2,1,0:T(8,128)} %get-tuple-element.213, pred[]{:T(512)S(6)} %compare.4, bf16[128,128,128]{2,0,1:T(8,128)(2,1)} %fusion.31, bf16[1,7,128,128]{3,2,1,0:T(8,128)(2,1)S(1)} %get-tuple-element.227, s32[]{:T(128)} %get-tuple-element.212), kind=kOutput, calls=%fused_computation.4.clone.1 | convolution fusion | flops 541065216 | bytes 21004292 | tf_op jit(solution)/shard_map/while/body/eval_jaxpr/bmps,bsn->bmpn/dot_general | solution.py:56
  359.4 5.5 fusion.31
  364.9 16.6 %bitcast_add_fusion.2 = f32[1,128,128,128]{3,2,1,0:T(8,128)} fusion(f32[1,128,128,128]{3,2,1,0:T(8,128)} %get-tuple-element.213, pred[]{:T(512)S(6)} %compare.4, bf16[128,128,128]{2,0,1:T(8,128)(2,1)} %fusion.31, bf16[1,7,128,128]{3,2,1,0:T(8,128)(2,1)S(1)} %get-tuple-element.227, s32[]{:T(128)} %get-tuple-element.212), kind=kOutput, calls=%fused_computation.4.clone.1 | convolution fusion | flops 541065216 | bytes 21004292 | tf_op jit(solution)/shard_map/while/body/eval_jaxpr/bmps,bsn->bmpn/dot_general | solution.py:56
  384.1 5.5 fusion.31
  389.5 16.6 %bitcast_add_fusion.2 = f32[1,128,128,128]{3,2,1,0:T(8,128)} fusion(f32[1,128,128,128]{3,2,1,0:T(8,128)} %get-tuple-element.213, pred[]{:T(512)S(6)} %compare.4, bf16[128,128,128]{2,0,1:T(8,128)(2,1)} %fusion.31, bf16[1,7,128,128]{3,2,1,0:T(8,128)(2,1)S(1)} %get-tuple-element.227, s32[]{:T(128)} %get-tuple-element.212), kind=kOutput, calls=%fused_computation.4.clone.1 | convolution fusion | flops 541065216 | bytes 21004292 | tf_op jit(solution)/shard_map/while/body/eval_jaxpr/bmps,bsn->bmpn/dot_general | solution.py:56
  406.2 6.4 bitcast_convert_fusion
  412.5 4.6 all-to-all-start
  417.2 4.7 copy.21
  421.9 44.9 %all-to-all-done = bf16[1,128,128,128]{3,2,0,1:T(8,128)(2,1)} async-done(((bf16[1,128,128,128]{3,2,0,1:T(8,128)(2,1)}), bf16[1,128,128,128]{3,2,0,1:T(8,128)(2,1)}, u32[]{:S(2)}, u32[]{:S(2)}) %all-to-all-start) | async-done | bytes 4194336 | tf_op jit(solution)/shard_map/all_to_all | solution.py:65
  466.8 2.7 copy.19
  470.2 6.0 bitcast_multiply_fusion
  476.4 217.0 %reduce-scatter.3.cloned.1.call-done = f32[1024,32]{0,1:T(8,128)} async-done(((f32[1024,1024]{0,1:T(8,128)}), f32[1024,32]{0,1:T(8,128)}) %reduce-scatter.3.cloned.1.call-update) | async-done | bytes 131088 | tf_op jit(solution)/shard_map/reduce_scatter | solution.py:76
  693.3 34.5 %reduce-scatter.5.cloned.1.call-done = f32[128,32]{0,1:T(8,128)} async-done(((f32[1024,32]{0,1:T(8,128)}), f32[128,32]{0,1:T(8,128)}) %reduce-scatter.5.cloned.1.call-update) | async-done | bytes 16400 | tf_op jit(solution)/shard_map/reduce_scatter | solution.py:77
  (43 shorter events, 9.6 us)
Async XLA Ops:
  6.5 19.7 %copy-start = (s32[160]{0:T(256)S(1)}, s32[160]{0:T(256)}, u32[]{:S(2)}) copy-start(s32[160]{0:T(256)} %param.13) | copy-start | bytes 1924
  6.5 144.0 %all-gather.5.cloned.1.call-start = ((), (), s32[]{:S(2)}) async-start(), calls=%async_computation.5 | async-start | bytes 5406720 | tf_op jit(solution)/shard_map/all_gather | solution.py:35
  7.3 225.7 %all-gather.3.cloned.1.call-start = ((), (), s32[]{:S(2)}) async-start(), calls=%async_computation.4 | async-start | bytes 5406720 | tf_op jit(solution)/shard_map/all_gather | solution.py:34
  14.9 124.0 %collective-permute-start = (bf16[1,128,128,128]{3,1,2,0:T(8,128)(2,1)}, bf16[1,128,128,128]{3,1,2,0:T(8,128)(2,1)}, u32[]{:S(2)}, u32[]{:S(2)}) collective-permute-start(bf16[1,128,128,128]{3,1,2,0:T(8,128)(2,1)} %copy.14), channel_id=1, source_target_pairs={{0,8},{8,16},{16,24},{24,32},{32,40},{40,48},{48,56},{56,64},{64,7... | collective-permute-start | bytes 12582920 | tf_op jit(solution)/shard_map/ppermute | solution.py:15
  16.8 123.3 %collective-permute-start.1 = (bf16[1,128,128,128]{3,1,2,0:T(8,128)(2,1)}, bf16[1,128,128,128]{3,1,2,0:T(8,128)(2,1)}, u32[]{:S(2)}, u32[]{:S(2)}) collective-permute-start(bf16[1,128,128,128]{3,1,2,0:T(8,128)(2,1)} %copy.14), channel_id=1, source_target_pairs={{8,0},{16,8},{24,16},{32,24},{40,32},{48,40},{56,48},{64,56},{72,6... | collective-permute-start | bytes 12582920 | tf_op jit(solution)/shard_map/ppermute | solution.py:18
  20.7 5.5 copy-start.3
  20.7 6.2 copy-start.4
  20.7 391.8 %all-to-all-start.1 = ((bf16[1,128,128,128]{3,2,0,1:T(8,128)(2,1)}), bf16[1,128,128,128]{3,2,0,1:T(8,128)(2,1)}, u32[]{:S(2)}, u32[]{:S(2)}) async-start(bf16[1,128,128,128]{3,2,0,1:T(8,128)(2,1)} %bitcast.64), calls=%async_computation.1 | async-start | bytes 8388608 | tf_op jit(solution)/shard_map/all_to_all | solution.py:39
  27.7 208.4 %copy-start.5 = (s32[1,7]{1,0:T(1,128)S(1)}, s32[1,7]{1,0:T(1,128)}, u32[]{:S(2)}) copy-start(s32[1,7]{1,0:T(1,128)} %param.14) | copy-start | bytes 88
  412.5 54.3 %all-to-all-start = ((bf16[1,128,128,128]{3,2,0,1:T(8,128)(2,1)}), bf16[1,128,128,128]{3,2,0,1:T(8,128)(2,1)}, u32[]{:S(2)}, u32[]{:S(2)}) async-start(bf16[1,128,128,128]{3,2,0,1:T(8,128)(2,1)} %bitcast_convert_fusion), calls=%async_computation | async-start | bytes 8388608 | tf_op jit(solution)/shard_map/all_to_all | solution.py:65
  417.1 276.2 %reduce-scatter.3.cloned.1.call-start = ((), (), s32[]{:S(2)}) async-start(), calls=%async_computation.6 | async-start | bytes 4325376 | tf_op jit(solution)/shard_map/reduce_scatter | solution.py:76
  466.8 3.4 copy-start.2
  470.2 257.6 %copy-start.1 = (s32[160]{0:T(256)S(1)}, s32[160]{0:T(256)}, u32[]{:S(2)}) copy-start(s32[160]{0:T(256)} %param.13) | copy-start | bytes 1924
  476.3 251.5 %reduce-scatter.5.cloned.1.call-start = ((), (), s32[]{:S(2)}) async-start(), calls=%async_computation.7 | async-start | bytes 147456 | tf_op jit(solution)/shard_map/reduce_scatter | solution.py:77
Sparse Core Ops, SparseCore 0:
  9.9 138.2 all-gather.4
  150.9 82.0 all-gather.2
  476.4 216.8 reduce-scatter.2
  695.8 31.9 reduce-scatter.4
where the time goes:
time: 735 us; the launch traced here: 734 us
  waiting for transfers between devices  489 us (67%)
  matrix products  158 us (21%)
  local copies, waits for them, and re-layouts  27 us (4%)
  other arithmetic  17 us (2%)
  starting transfers between devices  15.4 us (2%)
  between operations  13.9 us (2%)
  loops' own time  13.4 us (2%)
    reduce_scatter x1, waiting for transfers between devices, body(): lax.psum_scatter(partial_sum, 'pair', scatter_dimension=1, tiled=True)  217 us
    dot_general x7, matrix products, add_term(): jnp.einsum('bmps,bsn->bmpn', half_product, virt_tiles[:, slot_index], pre...  114 us
    ppermute x1, waiting for transfers between devices, padded(): lax.ppermute(lax.slice_in_dim(block, block.shape[dim] - width, None, axis...  111 us
    all_gather x1, waiting for transfers between devices, body(): lax.all_gather(green_occ, 'pair', axis=0, tiled=True)  79.2 us
    all_to_all x1, waiting for transfers between devices, body(): lax.all_to_all(products, 'aux', split_axis=1, concat_axis=2, tiled=True)  44.9 us
    dot_general x7, matrix products, add_term(): jnp.einsum('blm,blps->bmps', occ_tiles[:, slot_index], source_blocks, pre...  38.2 us
    reduce_scatter x1, waiting for transfers between devices, body(): lax.psum_scatter(columns, 'aux', scatter_dimension=0, tiled=True)  34.5 us
  transfers between devices with their start and end apart: 8, of which 6 were waited for; matrix products, arithmetic and copies ran while one was open for 26% of the time, Pallas kernels for 0%

commit v1 on v0

v1 whole, which is shorter than its diff:
```python
import functools
import math

import jax
import jax.numpy as jnp
from jax import lax
from jax.experimental import pallas as pl
from jax.experimental.pallas import tpu as pltpu
from jax.sharding import PartitionSpec as P

MESH = pl.DeviceIdType.MESH
BF = jnp.bfloat16
F32 = jnp.float32

BS = 128
NX, NZ, NY = 4, 8, 4
NPAIR = NX * NZ
NAUX = 2 * NY
SLOTS = 7
TILES = 5
PC = 16
CH = BS // PC
DEPTH = 3
GROUP = 2
QP = 4
ROWS = PC * NAUX
QX = 256
QZ = 32


def kernel(
    scale,
    t_hbm, occ_hbm, virt_hbm, home, src, tocc, tvirt, count,
    out,
    tv, xx, gocc, gvirt, sel, tiles, oo, tq, pt, pr, pq, pb, ar, bs, br, rr, cs, cr,
    t_sem, own_sem, bounce, z_ss, z_rs, x_ss, x_rs, s_ss, s_rs, s_own,
    h_ss, h_rs, q_ss, q_rs, q_own, p_ss, p_rs, p_own, a_ss, a_rs, a_own, b_ss, b_rs, b_own,
    c_ss, c_rs, c_own,
):
    k = lax.axis_index("pair")
    a = lax.axis_index("aux")
    x, z, y, c = k // NZ, lax.rem(k, NZ), a // 2, lax.rem(a, 2)
    up, down = lax.rem(k + 1, NPAIR), lax.rem(k + NPAIR - 1, NPAIR)

    def aux_peer(d):
        return lax.rem(a + d, NAUX)

    def z_peer(d):
        return x * NZ + lax.rem(z + d, NZ)

    def x_peer(d):
        return lax.rem(x + d, NX) * NZ + z

    def remote(s, d, ss, rs, dev):
        return pltpu.make_async_remote_copy(
            src_ref=s, dst_ref=d, send_sem=ss, recv_sem=rs, device_id=dev, device_id_type=MESH
        )

    def load(i):
        return pltpu.make_async_copy(
            t_hbm.at[0, :, pl.ds(i * PC, PC), :], tv.at[i], t_sem.at[i]
        )

    myrows = pl.ds(pl.multiple_of(a * 16, 16), 16)

    def tile_z(kind, d):
        hbm, g = ((occ_hbm, gocc), (virt_hbm, gvirt))[kind]
        return remote(
            hbm.at[:, myrows, :], g.at[pl.ds(k * TILES, TILES)],
            z_ss.at[kind, d], z_rs.at[kind, d], (z_peer(d), a),
        )

    def tile_own(kind):
        hbm, g = ((occ_hbm, gocc), (virt_hbm, gvirt))[kind]
        return pltpu.make_async_copy(
            hbm.at[:, myrows, :], g.at[pl.ds(k * TILES, TILES)], own_sem.at[kind]
        )

    def tile_x(kind, d):
        g = (gocc, gvirt)[kind]
        part = pl.ds(x * NZ * TILES, NZ * TILES)
        return remote(
            g.at[part], g.at[part], x_ss.at[kind, d], x_rs.at[kind, d], (x_peer(d), a)
        )

    def tile_s(d):
        return remote(
            sel, tiles.at[:, myrows, :], s_ss.at[d], s_rs.at[d], (k, aux_peer(d))
        )

    def halo(i, side):
        part = pl.ds(i * PC, PC)
        return remote(
            xx.at[1, part], xx.at[2 * side, part],
            h_ss.at[side, i], h_rs.at[side, i], ((down if side else up), a),
        )

    def rows_q(d, part):
        b = aux_peer(d)
        w = BS // QP
        return remote(
            t_hbm.at[0, pl.ds(b * 16, 16), pl.ds(part * w, w), :],
            tq.at[:, pl.ds(pl.multiple_of(a * BS + part * w, 16), w), :],
            q_ss.at[d, part], q_rs.at[d, part], (k, b),
        )

    def rows_own():
        return pltpu.make_async_copy(
            t_hbm.at[0, pl.ds(a * 16, 16)],
            tq.at[:, pl.ds(pl.multiple_of(a * BS, BS), BS), :], q_own.at[0],
        )

    prow = pl.ds(pl.multiple_of((c * NY + y) * PC, PC), PC)

    def prod_s(i, d):
        b = aux_peer(d)
        return remote(
            pr.at[i, pl.ds(b * 16, 16)], pq.at[i, :, prow, :],
            p_ss.at[i, d], p_rs.at[i, d], (k, b),
        )

    def prod_own(i):
        return pltpu.make_async_copy(
            pr.at[i, pl.ds(a * 16, 16)], pq.at[i, :, prow, :], p_own.at[i]
        )

    def part_a(i, e):
        dx, dc = e // 2, e % 2
        cc = lax.rem(c + dc, 2)
        return remote(
            pb.at[i, lax.rem(x + dx, NX), pl.ds(pl.multiple_of(cc * 64, 64), 64), :],
            ar.at[i, e], a_ss.at[i, e], a_rs.at[i, e], (x_peer(dx), y * 2 + cc),
        )

    def part_a_own(i):
        return pltpu.make_async_copy(
            pb.at[i, x, pl.ds(pl.multiple_of(c * 64, 64), 64), :], ar.at[i, 0], a_own.at[i]
        )

    def part_b(i, d):
        yy = lax.rem(y + d, NY)
        return remote(
            bs.at[i, pl.ds(pl.multiple_of(yy * PC, PC), PC), :], br.at[i, d],
            b_ss.at[i, d], b_rs.at[i, d], (k, yy * 2 + c),
        )

    def part_b_own(i):
        return pltpu.make_async_copy(
            bs.at[i, pl.ds(pl.multiple_of(y * PC, PC), PC), :], br.at[i, 0], b_own.at[i]
        )

    def part_c(d):
        zz = lax.rem(z + d, NZ)
        return remote(
            cs.at[pl.ds(pl.multiple_of(zz * QZ, QZ), QZ), :], cr.at[d],
            c_ss.at[d], c_rs.at[d], (z_peer(d), a),
        )

    def part_c_own():
        return pltpu.make_async_copy(
            cs.at[pl.ds(pl.multiple_of(z * QZ, QZ), QZ), :], cr.at[0], c_own.at[0]
        )

    def turn(i):
        load(i).wait()
        xx[1, pl.ds(i * PC, PC)] = jnp.swapaxes(tv[i], 0, 1)

    def start_load(i, carry):
        load(i).start()
        return carry

    lax.fori_loop(0, CH, start_load, 0)
    for kind in range(2):
        tile_own(kind).start()
    rows_own().start()
    barrier = pltpu.get_barrier_semaphore()
    partners = [(up, a), (down, a)]
    partners += [(k, aux_peer(d)) for d in range(1, NAUX)]
    partners += [(z_peer(d), a) for d in range(1, NZ)]
    partners += [
        (x_peer(d), y * 2 + lax.rem(c + dc, 2)) for d in range(1, NX) for dc in range(2)
    ]
    for dev in partners:
        pl.semaphore_signal(barrier, inc=1, device_id=dev, device_id_type=MESH)
    turn(0)
    pl.semaphore_wait(barrier, len(partners))

    def send_halo(i):
        for side in range(2):
            halo(i, side).start()

    def send_rows(part):
        for d in range(1, NAUX):
            rows_q(d, part).start()

    for kind in range(2):
        for d in range(1, NZ):
            tile_z(kind, d).start()
    send_halo(0)
    send_rows(0)

    def first(i, carry):
        turn(i)
        send_halo(i)
        return carry

    lax.fori_loop(1, DEPTH, first, 0)

    def rest(i, carry):
        turn(i)
        return carry

    lax.fori_loop(DEPTH, CH, rest, 0)
    for kind in range(2):
        tile_own(kind).wait()
        for d in range(1, NZ):
            tile_z(kind, d).wait_recv()
    for kind in range(2):
        for d in range(1, NX):
            tile_x(kind, d).start()
    send_rows(1)
    for kind in range(2):
        for d in range(1, NX):
            tile_x(kind, d).wait_recv()
    for j in range(SLOTS):
        sel[j] = gocc[home[tocc[0, j]]]
        sel[SLOTS + j] = gvirt[home[tvirt[0, j]]]
    for d in range(1, NAUX):
        tile_s(d).start()
    keep = pltpu.make_async_copy(sel, tiles.at[:, myrows, :], s_own.at[0])
    keep.start()
    keep.wait()
    for d in range(1, NAUX):
        tile_s(d).wait_recv()

    live = count[0]
    for j in range(SLOTS):
        turned = tiles[j].astype(F32).T
        for s in range(3):
            weight = jnp.where(jnp.logical_and(src[0, j] == s, j < live), 1.0, 0.0)
            oo[pl.ds(j * BS, BS), pl.ds(s * BS, BS)] = (turned * weight).astype(BF)

    def products(i):
        for side in range(2):
            halo(i, side).wait_recv()

        @pl.when(i + DEPTH < CH)
        def _():
            send_halo(i + DEPTH)

        @pl.when(i + 2 < QP)
        def _():
            send_rows(i + 2)

        def group(g, carry):
            p0 = i * PC + g * GROUP
            stacked = jnp.concatenate(
                [
                    jnp.concatenate([xx[s, p0 + u] for u in range(GROUP)], axis=1)
                    for s in range(3)
                ],
                axis=0,
            )
            half = jnp.dot(oo[...], stacked, preferred_element_type=F32).astype(BF)
            side = jnp.concatenate(
                [
                    jnp.concatenate(
                        [
                            half[j * BS:(j + 1) * BS, u * BS:(u + 1) * BS]
                            for j in range(SLOTS)
                        ],
                        axis=1,
                    )
                    for u in range(GROUP)
                ],
                axis=0,
            )
            virt = tiles[pl.ds(SLOTS, SLOTS)].reshape(SLOTS * BS, BS)
            prod = jnp.dot(side, virt, preferred_element_type=F32).astype(BF)
            pt[pl.ds(g * GROUP, GROUP)] = prod.reshape(GROUP, BS, BS)
            return carry

        lax.fori_loop(0, PC // GROUP, group, 0)
        pr[i] = jnp.swapaxes(pt[...], 0, 1)
        prod_own(i).start()
        for d in range(1, NAUX):
            prod_s(i, d).start()

    def contract(i):
        prod_own(i).wait()
        for d in range(1, NAUX):
            prod_s(i, d).wait_recv()

        def block(n, carry):
            left = jnp.concatenate([pq[i, m] for m in range(16)], axis=1)
            qs = pl.ds(pl.multiple_of(n * QX, QX), QX)
            right = jnp.concatenate([tq[m, qs, :] for m in range(16)], axis=1)
            pb[i, n] = lax.dot_general(
                left, right, (((1,), (1,)), ((), ())), preferred_element_type=F32
            ).astype(BF)
            return carry

        lax.fori_loop(0, NX, block, 0)
        part_a_own(i).start()
        for e in range(1, 2 * NX):
            part_a(i, e).start()

    def add_a(i):
        part_a_own(i).wait()
        for e in range(1, 2 * NX):
            part_a(i, e).wait_recv()
        total = ar[i, 0].astype(F32)
        for e in range(1, 2 * NX):
            total = total + ar[i, e].astype(F32)
        bs[i] = total
        part_b_own(i).start()
        for d in range(1, NY):
            part_b(i, d).start()

    def add_b(i):
        part_b_own(i).wait()
        for d in range(1, NY):
            part_b(i, d).wait_recv()
        total = br[i, 0]
        for d in range(1, NY):
            total = total + br[i, d]
        rr[pl.ds(pl.multiple_of(i * PC, PC), PC), :] = total

    def step(i, carry):
        @pl.when(i < CH)
        def _():
            products(i)

        @pl.when(i == 1)
        def _():
            rows_own().wait()
            for part in range(QP):
                for d in range(1, NAUX):
                    rows_q(d, part).wait_recv()

        @pl.when(jnp.logical_and(i >= 1, i <= CH))
        def _():
            contract(i - 1)

        @pl.when(jnp.logical_and(i >= 2, i <= CH + 1))
        def _():
            add_a(i - 2)

        @pl.when(i >= 3)
        def _():
            add_b(i - 3)

        return carry

    lax.fori_loop(0, CH + 3, step, 0)

    cs[...] = rr[...].T
    part_c_own().start()
    for d in range(1, NZ):
        part_c(d).start()
    part_c_own().wait()
    for d in range(1, NZ):
        part_c(d).wait_recv()
    total = cr[0]
    for d in range(1, NZ):
        total = total + cr[d]
    out[...] = total.T * scale

    for kind in range(2):
        for d in range(1, NZ):
            tile_z(kind, d).wait_send()
        for d in range(1, NX):
            tile_x(kind, d).wait_send()
    for d in range(1, NAUX):
        tile_s(d).wait_send()
        for part in range(QP):
            rows_q(d, part).wait_send()

    def drain(i, carry):
        for side in range(2):
            halo(i, side).wait_send()
        for d in range(1, NAUX):
            prod_s(i, d).wait_send()
        for e in range(1, 2 * NX):
            part_a(i, e).wait_send()
        for d in range(1, NY):
            part_b(i, d).wait_send()
        return carry

    lax.fori_loop(0, CH, drain, 0)
    for d in range(1, NZ):
        part_c(d).wait_send()


def body(three_centre, green_occ, green_virt, tile_home, term_source, term_occ, term_virt, term_count):
    vm = pltpu.VMEM
    dma = pltpu.SemaphoreType.DMA
    scale = -1.0 / (BS * math.sqrt(NPAIR * SLOTS))
    hbm = pl.BlockSpec(memory_space=pl.ANY)
    smem = pl.BlockSpec(memory_space=pltpu.SMEM)
    return pl.pallas_call(
        functools.partial(kernel, scale),
        out_shape=jax.ShapeDtypeStruct((BS, QZ), F32),
        in_specs=[hbm] * 3 + [smem] * 5,
        out_specs=pl.BlockSpec(memory_space=pltpu.VMEM),
        scratch_shapes=[
            vm((CH, BS, PC, BS), BF),
            vm((3, BS, BS, BS), BF),
            vm((NPAIR * TILES, 16, BS), BF),
            vm((NPAIR * TILES, 16, BS), BF),
            vm((2 * SLOTS, 16, BS), BF),
            vm((2 * SLOTS, BS, BS), BF),
            vm((SLOTS * BS, 3 * BS), BF),
            vm((16, NAUX * BS, BS), BF),
            vm((PC, BS, BS), BF),
            vm((CH, BS, PC, BS), BF),
            vm((CH, 16, ROWS, BS), BF),
            vm((CH, NX, ROWS, QX), BF),
            vm((CH, 2 * NX, 64, QX), BF),
            vm((CH, 64, QX), F32),
            vm((CH, NY, PC, QX), F32),
            vm((BS, QX), F32),
            vm((QX, BS), F32),
            vm((NZ, QZ, BS), F32),
            dma((CH,)), dma((2,)), dma((1,)),
            dma((2, NZ)), dma((2, NZ)), dma((2, NX)), dma((2, NX)),
            dma((NAUX,)), dma((NAUX,)), dma((1,)),
            dma((2, CH)), dma((2, CH)),
            dma((NAUX, QP)), dma((NAUX, QP)), dma((1,)),
            dma((CH, NAUX)), dma((CH, NAUX)), dma((CH,)),
            dma((CH, 2 * NX)), dma((CH, 2 * NX)), dma((CH,)),
            dma((CH, NY)), dma((CH, NY)), dma((CH,)),
            dma((NZ,)), dma((NZ,)), dma((1,)),
        ],
        compiler_params=pltpu.CompilerParams(
            collective_id=0, has_side_effects=True, vmem_limit_bytes=60 * 2**20
        ),
    )(three_centre, green_occ, green_virt, tile_home, term_source, term_occ, term_virt, term_count)


def solution(mesh):
    in_specs = (
        P("pair", None, "aux", None),
        P("pair", None, None),
        P("pair", None, None),
        P(),
        P("pair", None),
        P("pair", None),
        P("pair", None),
        P("pair"),
    )
    return jax.shard_map(
        body, mesh=mesh, in_specs=in_specs, out_specs=P("aux", "pair"), check_vma=False
    )
```

time: 735 us -> 217 us (0.30)
  waiting for transfers between devices: 489 us -> 0 us
  Pallas kernels: 0 us -> 213 us
  matrix products: 158 us -> 0 us
  local copies, waits for them, and re-layouts: 27 us -> 1.52 us
  other arithmetic: 17 us -> 0 us
  starting transfers between devices: 15.4 us -> 0 us
  loops' own time: 13.4 us -> 0 us
  between operations: 13.9 us -> 0.66 us
    reduce_scatter x2 -> x0, waiting for transfers between devices: 251 us -> none  [the longest x1 217 us: body(): lax.psum_scatter(partial_sum, 'pair', scatter_dimension=1, tiled=True)]
    pallas_call x0 -> x1, Pallas kernels: none -> 213 us  [body(): pl.pallas_call(functools.partial(kernel, scale), out_shape=jax.ShapeDtype...]
    dot_general x15 -> x0, matrix products: 158 us -> none  [the longest x7 114 us: add_term(): jnp.einsum('bmps,bsn->bmpn', half_product, virt_tiles[:, slot_index], pre...]
    ppermute x2 -> x0, waiting for transfers between devices: 112 us -> none  [the longest x1 111 us: padded(): lax.ppermute(lax.slice_in_dim(block, block.shape[dim] - width, None, axis...]
    all_gather x2 -> x0, waiting for transfers between devices: 79.2 us -> none  [the longest x1 79.2 us: body(): lax.all_gather(green_occ, 'pair', axis=0, tiled=True)]
    all_to_all x2 -> x0, waiting for transfers between devices: 44.9 us -> none  [the longest x1 44.9 us: body(): lax.all_to_all(products, 'aux', split_axis=1, concat_axis=2, tiled=True)]
    another operation x1 -> x0, loops' own time: 13.4 us -> none  [body(): lax.fori_loop(0, slot_total, add_term, start).astype(jnp.bfloat16)]
    concatenate x1 -> x0, other arithmetic: 10.5 us -> none  [padded(): block = jnp.concatenate([low, block, high], axis=dim)]
  transfers between devices with their start and end apart: 8 -> 0, of which waited for: 6 -> 0; matrix products, arithmetic and copies ran while one was open for 26% -> 0% of each run, Pallas kernels for 0% -> 0%
where the time goes in v1:
time: 217 us; the launch traced here: 215 us
  Pallas kernels  213 us (98%)
    pallas_call x1, Pallas kernels, body(): pl.pallas_call(functools.partial(kernel, scale), out_shape=jax.ShapeDtype...  213 us

profile of v1, /device:TPU:2, one launch (start us, length us, event | category | flops | bytes accessed | tf_op | source)
XLA Modules:
  0.0 215.0 jit_solution(1937296527847193390)
XLA Ops:
  0.7 212.9 %shard_map.82 = f32[128,32]{1,0:T(8,128)} custom-call(bf16[1,128,128,128]{3,2,1,0:T(8,128)(2,1)} %t_hbm.1, bf16[5,128,128]{2,1,0:T(8,128)(2,1)} %occ_hbm.1, bf16[5,128,128]{2,1,0:T(8,128)(2,1)} %virt_hbm.1, s32[160]{0:T(256)} %home.1, s32[1,7]{1,0:T(1,128)} %src.1, s32[1,7]{1,0:T(1,128)} %tocc.1, s32[1,7]{1,0:T(1,128)} %tvirt.1, s32[1]{0:T(128)S(6)} %copy.10.count), custom_call_target="tpu_custom_call" | custom-call | tf_op jit(solution)/shard_map/pallas_call | solution.py:401
  213.5 1.5 copy.9

commit v2 on v1

--- a/solution.py
+++ b/solution.py
@@ -21,6 +21,8 @@
 PC = 16
 CH = BS // PC
 DEPTH = 3
+EARLY = 5
+LAG = 3
 GROUP = 2
 QP = 4
 ROWS = PC * NAUX
@@ -32,8 +34,8 @@
     scale,
     t_hbm, occ_hbm, virt_hbm, home, src, tocc, tvirt, count,
     out,
-    tv, xx, gocc, gvirt, sel, tiles, oo, tq, pt, pr, pq, pb, ar, bs, br, rr, cs, cr,
-    t_sem, own_sem, bounce, z_ss, z_rs, x_ss, x_rs, s_ss, s_rs, s_own,
+    tv, xx, gocc, gvirt, ask, asked, given, got, sel, tiles, oo, tq, pt, pr, pq, pb, ar, bs, br, rr, cs, cr,
+    bounce, t_sem, own_sem, e_ss, e_rs, f_ss, z_ss, z_rs, w_ss, w_rs, x_ss, x_rs, s_ss, s_rs, s_own,
     h_ss, h_rs, q_ss, q_rs, q_own, p_ss, p_rs, p_own, a_ss, a_rs, a_own, b_ss, b_rs, b_own,
     c_ss, c_rs, c_own,
 ):
@@ -66,21 +68,22 @@
     def tile_z(kind, d):
         hbm, g = ((occ_hbm, gocc), (virt_hbm, gvirt))[kind]
         return remote(
-            hbm.at[:, myrows, :], g.at[pl.ds(k * TILES, TILES)],
+            hbm.at[:, myrows, :], g.at[pl.ds(z * TILES, TILES)],
             z_ss.at[kind, d], z_rs.at[kind, d], (z_peer(d), a),
         )
 
     def tile_own(kind):
         hbm, g = ((occ_hbm, gocc), (virt_hbm, gvirt))[kind]
         return pltpu.make_async_copy(
-            hbm.at[:, myrows, :], g.at[pl.ds(k * TILES, TILES)], own_sem.at[kind]
-        )
-
-    def tile_x(kind, d):
-        g = (gocc, gvirt)[kind]
-        part = pl.ds(x * NZ * TILES, NZ * TILES)
-        return remote(
-            g.at[part], g.at[part], x_ss.at[kind, d], x_rs.at[kind, d], (x_peer(d), a)
+            hbm.at[:, myrows, :], g.at[pl.ds(z * TILES, TILES)], own_sem.at[kind]
+        )
+
+    def wish(d):
+        return remote(ask.at[0], ask.at[d], w_ss.at[d], w_rs.at[d], (x_peer(d), a))
+
+    def tile_x(d):
+        return remote(
+            given.at[d], got.at[d], x_ss.at[d], x_rs.at[d], (x_peer(NX - d), a)
         )
 
     def tile_s(d):
@@ -94,6 +97,36 @@
             xx.at[1, part], xx.at[2 * side, part],
             h_ss.at[side, i], h_rs.at[side, i], ((down if side else up), a),
         )
+
+    edge = jnp.logical_or(z == 0, z == NZ - 1)
+    at_top = z // (NZ - 1)
+    edge_side = 1 - at_top
+    beyond = lax.rem(x + NX + 2 * at_top - 1, NX) * NZ + z
+
+    def halo_half(i, side):
+        part = pl.ds(i * PC, PC // 2)
+        return remote(
+            xx.at[1, part], xx.at[2 * side, part],
+            h_ss.at[side, i], h_rs.at[side, i], ((down if side else up), a),
+        )
+
+    def halo_away(i):
+        return remote(
+            xx.at[1, pl.ds(i * PC + PC // 2, PC // 2)], bounce.at[i],
+            e_ss.at[i], e_rs.at[i], (beyond, a),
+        )
+
+    def halo_on(i):
+        return remote(
+            bounce.at[i], xx.at[2 * edge_side, pl.ds(i * PC + PC // 2, PC // 2)],
+            f_ss.at[i], h_rs.at[edge_side, i], (x * NZ + NZ - 1 - z, a),
+        )
+
+    def send_on(i):
+        @pl.when(edge)
+        def _():
+            halo_away(i).wait_recv()
+            halo_on(i).start()
 
     def rows_q(d, part):
         b = aux_peer(d)
@@ -182,57 +215,90 @@
     ]
     for dev in partners:
         pl.semaphore_signal(barrier, inc=1, device_id=dev, device_id_type=MESH)
+    lane = lax.broadcasted_iota(jnp.int32, (8, BS), 1)
+    wanted = jnp.zeros((8, BS), jnp.int32)
+    for j in range(SLOTS):
+        wanted = jnp.where(lane == j, home[tocc[0, j]], wanted)
+        wanted = jnp.where(lane == SLOTS + j, home[tvirt[0, j]], wanted)
+    ask[0] = wanted
     turn(0)
     pl.semaphore_wait(barrier, len(partners))
 
     def send_halo(i):
-        for side in range(2):
-            halo(i, side).start()
+        for side, last in ((0, NZ - 1), (1, 0)):
+
+            @pl.when(z == last)
+            def _():
+                halo_half(i, side).start()
+                halo_away(i).start()
+
+            @pl.when(z != last)
+            def _():
+                halo(i, side).start()
 
     def send_rows(part):
         for d in range(1, NAUX):
             rows_q(d, part).start()
 
+    for d in range(1, NX):
+        wish(d).start()
     for kind in range(2):
         for d in range(1, NZ):
             tile_z(kind, d).start()
+    send_rows(0)
     send_halo(0)
-    send_rows(0)
-
-    def first(i, carry):
-        turn(i)
-        send_halo(i)
-        return carry
-
-    lax.fori_loop(1, DEPTH, first, 0)
 
     def rest(i, carry):
         turn(i)
         return carry
 
-    lax.fori_loop(DEPTH, CH, rest, 0)
+    lax.fori_loop(1, CH, rest, 0)
+    for d in range(1, NX):
+        wish(d).wait_recv()
+    read = pltpu.make_async_copy(ask, asked, s_own.at[1])
+    read.start()
+    read.wait()
     for kind in range(2):
         tile_own(kind).wait()
         for d in range(1, NZ):
             tile_z(kind, d).wait_recv()
-    for kind in range(2):
-        for d in range(1, NX):
-            tile_x(kind, d).start()
-    send_rows(1)
-    for kind in range(2):
-        for d in range(1, NX):
-            tile_x(kind, d).wait_recv()
-    for j in range(SLOTS):
-        sel[j] = gocc[home[tocc[0, j]]]
-        sel[SLOTS + j] = gvirt[home[tvirt[0, j]]]
+    for d in range(NX):
+        for j in range(2 * SLOTS):
+            g = gocc if j < SLOTS else gvirt
+            row = jnp.clip(asked[d, 0, j] - x * (NZ * TILES), 0, NZ * TILES - 1)
+            if d == 0:
+                got[0, j] = g[row]
+            else:
+                given[d, j] = g[row]
+        if d > 0:
+            tile_x(d).start()
+
+    def first(i, carry):
+        send_halo(i)
+        return carry
+
+    lax.fori_loop(1, DEPTH, first, 0)
+    send_on(0)
+    for d in range(1, NX):
+        tile_x(d).wait_recv()
+    for j in range(2 * SLOTS):
+        owner = asked[0, 0, j] // (NZ * TILES)
+        sel[j] = got[lax.rem(owner + NX - x, NX), j]
     for d in range(1, NAUX):
         tile_s(d).start()
     keep = pltpu.make_async_copy(sel, tiles.at[:, myrows, :], s_own.at[0])
     keep.start()
     keep.wait()
+    send_rows(1)
+    for i in range(1, DEPTH - 1):
+        send_on(i)
+    for i in range(DEPTH, EARLY):
+        send_halo(i)
     for d in range(1, NAUX):
         tile_s(d).wait_recv()
 
+    for part in range(2, QP):
+        send_rows(part)
     live = count[0]
     for j in range(SLOTS):
         turned = tiles[j].astype(F32).T
@@ -241,16 +307,16 @@
             oo[pl.ds(j * BS, BS), pl.ds(s * BS, BS)] = (turned * weight).astype(BF)
 
     def products(i):
+        @pl.when(i + DEPTH - 1 < CH)
+        def _():
+            send_on(i + DEPTH - 1)
+
         for side in range(2):
             halo(i, side).wait_recv()
 
-        @pl.when(i + DEPTH < CH)
+        @pl.when(jnp.logical_and(i + DEPTH >= EARLY, i + DEPTH < CH))
         def _():
             send_halo(i + DEPTH)
-
-        @pl.when(i + 2 < QP)
-        def _():
-            send_rows(i + 2)
 
         def group(g, carry):
             p0 = i * PC + g * GROUP
@@ -331,28 +397,28 @@
         def _():
             products(i)
 
-        @pl.when(i == 1)
+        @pl.when(i == LAG)
         def _():
             rows_own().wait()
             for part in range(QP):
                 for d in range(1, NAUX):
                     rows_q(d, part).wait_recv()
 
-        @pl.when(jnp.logical_and(i >= 1, i <= CH))
-        def _():
-            contract(i - 1)
-
-        @pl.when(jnp.logical_and(i >= 2, i <= CH + 1))
-        def _():
-            add_a(i - 2)
-
-        @pl.when(i >= 3)
-        def _():
-            add_b(i - 3)
+        @pl.when(jnp.logical_and(i >= LAG, i < CH + LAG))
+        def _():
+            contract(i - LAG)
+
+        @pl.when(jnp.logical_and(i >= LAG + 1, i < CH + LAG + 1))
+        def _():
+            add_a(i - LAG - 1)
+
+        @pl.when(i >= LAG + 2)
+        def _():
+            add_b(i - LAG - 2)
 
         return carry
 
-    lax.fori_loop(0, CH + 3, step, 0)
+    lax.fori_loop(0, CH + LAG + 2, step, 0)
 
     cs[...] = rr[...].T
     part_c_own().start()
@@ -369,16 +435,27 @@
     for kind in range(2):
         for d in range(1, NZ):
             tile_z(kind, d).wait_send()
-        for d in range(1, NX):
-            tile_x(kind, d).wait_send()
+    for d in range(1, NX):
+        wish(d).wait_send()
+        tile_x(d).wait_send()
     for d in range(1, NAUX):
         tile_s(d).wait_send()
         for part in range(QP):
             rows_q(d, part).wait_send()
 
     def drain(i, carry):
-        for side in range(2):
-            halo(i, side).wait_send()
+        for side, last in ((0, NZ - 1), (1, 0)):
+
+            @pl.when(z == last)
+            def _():
+                halo_half(i, side).wait_send()
+                halo_away(i).wait_send()
+                halo_on(i).wait_send()
+
+            @pl.when(z != last)
+            def _():
+                halo(i, side).wait_send()
+
         for d in range(1, NAUX):
             prod_s(i, d).wait_send()
         for e in range(1, 2 * NX):
@@ -406,8 +483,12 @@
         scratch_shapes=[
             vm((CH, BS, PC, BS), BF),
             vm((3, BS, BS, BS), BF),
-            vm((NPAIR * TILES, 16, BS), BF),
-            vm((NPAIR * TILES, 16, BS), BF),
+            vm((NZ * TILES, 16, BS), BF),
+            vm((NZ * TILES, 16, BS), BF),
+            vm((NX, 8, BS), jnp.int32),
+            pltpu.SMEM((NX, 8, BS), jnp.int32),
+            vm((NX, 2 * SLOTS, 16, BS), BF),
+            vm((NX, 2 * SLOTS, 16, BS), BF),
             vm((2 * SLOTS, 16, BS), BF),
             vm((2 * SLOTS, BS, BS), BF),
             vm((SLOTS * BS, 3 * BS), BF),
@@ -422,9 +503,10 @@
             vm((BS, QX), F32),
             vm((QX, BS), F32),
             vm((NZ, QZ, BS), F32),
-            dma((CH,)), dma((2,)), dma((1,)),
-            dma((2, NZ)), dma((2, NZ)), dma((2, NX)), dma((2, NX)),
-            dma((NAUX,)), dma((NAUX,)), dma((1,)),
+            vm((CH, PC // 2, BS, BS), BF),
+            dma((CH,)), dma((2,)), dma((CH,)), dma((CH,)), dma((CH,)),
+            dma((2, NZ)), dma((2, NZ)), dma((NX,)), dma((NX,)), dma((NX,)), dma((NX,)),
+            dma((NAUX,)), dma((NAUX,)), dma((2,)),
             dma((2, CH)), dma((2, CH)),
             dma((NAUX, QP)), dma((NAUX, QP)), dma((1,)),
             dma((CH, NAUX)), dma((CH, NAUX)), dma((CH,)),

time: 217 us -> 159 us (0.73)
  Pallas kernels: 213 us -> 156 us
    pallas_call x1, Pallas kernels: 213 us -> 156 us  [body(): pl.pallas_call(functools.partial(kernel, scale), out_shape=jax.ShapeDtype...]
where the time goes in v2:
time: 159 us; the launch traced here: 158 us
  Pallas kernels  156 us (98%)
    pallas_call x1, Pallas kernels, body(): pl.pallas_call(functools.partial(kernel, scale), out_shape=jax.ShapeDtype...  156 us

profile of v2, /device:TPU:2, one launch (start us, length us, event | category | flops | bytes accessed | tf_op | source)
XLA Modules:
  0.0 157.8 jit_solution(10718461537703014596)
XLA Ops:
  0.7 155.7 %shard_map.82 = f32[128,32]{1,0:T(8,128)} custom-call(bf16[1,128,128,128]{3,2,1,0:T(8,128)(2,1)} %t_hbm.1, bf16[5,128,128]{2,1,0:T(8,128)(2,1)} %occ_hbm.1, bf16[5,128,128]{2,1,0:T(8,128)(2,1)} %virt_hbm.1, s32[160]{0:T(256)} %home.1, s32[1,7]{1,0:T(1,128)} %src.1, s32[1,7]{1,0:T(1,128)} %tocc.1, s32[1,7]{1,0:T(1,128)} %tvirt.1, s32[1]{0:T(128)S(6)} %copy.10.count), custom_call_target="tpu_custom_call" | custom-call | tf_op jit(solution)/shard_map/pallas_call | solution.py:478
  156.3 1.5 copy.9
